TPU v7x, 128 devices: a whole 4x4x4 slice. The times are simulated.
128 devices in a mesh: seq: 8 (over y, core), tensor: 16 (over x, z).
Axes of the slice: x: 4, y: 4, z: 4, core: 2. Of those that a mesh axis runs over, the one named last changes fastest.
Arguments:
- tokens: bfloat16 [16384, 4096], P('seq', 'tensor'), may hold values from -6 to 6
- w_query: bfloat16 [4096, 4096], P(None, 'tensor'), may hold values from -0.09375 to 0.09375
- w_key: bfloat16 [4096, 4096], P(None, 'tensor'), may hold values from -0.09375 to 0.09375
- w_value: bfloat16 [4096, 4096], P(None, 'tensor'), may hold values from -0.09375 to 0.09375
- w_output: bfloat16 [4096, 4096], P('tensor'), may hold values from -0.09375 to 0.09375
Outputs:
- mixed: bfloat16 [16384, 4096], P('seq', 'tensor')
All inputs are finite; a program needn't handle non-finite values.
Results may differ from a plain program's by a relative error of at most 0.023.
Values may be sent and summed in bfloat16 or wider, within the bound.
A program may use at most 128 MiB of HBM per device.

v0:
```python
import math

import jax
import jax.numpy as jnp
from jax import lax
from jax.sharding import PartitionSpec as P

DH = 128
BLOCK = 256


def carried_in(array, axis, combine, identity):
    count, index = (lax.axis_size(axis), lax.axis_index(axis))
    everything = lax.all_gather(array.astype(jnp.bfloat16), axis)
    start = jnp.broadcast_to(jnp.asarray(identity, array.dtype), array.shape)

    def step(k, before):
        reached = k < index
        new = combine(before, everything[k].astype(array.dtype))
        return jnp.where(reached, new, before)

    return lax.fori_loop(0, count, step, start)


def add_states(earlier, later):
    return earlier + later


def local(tokens, w_query, w_key, w_value, w_output):
    tok_rows = tokens.shape[0]
    local_width = w_query.shape[1]
    local_heads = local_width // DH
    block_count = tok_rows // BLOCK
    att_scale = 1.0 / math.sqrt(DH * tok_rows * lax.axis_size("seq"))
    shard_piece = lax.all_gather(tokens, "tensor", axis=1, tiled=True)
    query_sum, key_sum, value_sum = tuple(
        (
            jnp.dot(shard_piece, weight, preferred_element_type=jnp.float32)
            for weight in (w_query, w_key, w_value)
        )
    )
    shape_blocks = (block_count, BLOCK, local_heads, DH)
    query = query_sum.astype(jnp.bfloat16).reshape(shape_blocks)
    key_all = key_sum.astype(jnp.bfloat16).reshape(shape_blocks)
    value_all = value_sum.astype(jnp.bfloat16).reshape(shape_blocks)
    block_states = jnp.einsum(
        "nbhd,nbhe->nhde", key_all, value_all, preferred_element_type=jnp.float32
    )
    running = jnp.cumsum(block_states, axis=0)
    local_total = running[-1]
    carry_in = carried_in(local_total, "seq", add_states, jnp.zeros_like(local_total))
    before = jnp.concatenate(
        [jnp.zeros((1,) + local_total.shape, jnp.float32), running[:-1]], axis=0
    )
    before_low = (carry_in[None] + before).astype(jnp.bfloat16)
    inter = jnp.einsum("nbhd,nhde->nbhe", query, before_low, preferred_element_type=jnp.float32)
    scores = jnp.einsum("nbhd,nchd->nhbc", query, key_all, preferred_element_type=jnp.float32)
    causal_mask = jnp.arange(BLOCK)[:, None] >= jnp.arange(BLOCK)[None, :]
    scores_low = jnp.where(causal_mask[None, None], scores, jnp.float32(0.0)).astype(jnp.bfloat16)
    intra = jnp.einsum("nhbc,nche->nbhe", scores_low, value_all, preferred_element_type=jnp.float32)
    attended = ((inter + intra) * att_scale).astype(jnp.bfloat16).reshape(tok_rows, local_width)
    partial_out = jnp.dot(attended, w_output, preferred_element_type=jnp.float32)
    return lax.psum_scatter(
        partial_out.astype(jnp.bfloat16), "tensor", scatter_dimension=1, tiled=True
    )


def solution(mesh):
    in_specs = (
        P("seq", "tensor"),
        P(None, "tensor"),
        P(None, "tensor"),
        P(None, "tensor"),
        P("tensor", None),
    )
    out_specs = P("seq", "tensor")
    return jax.shard_map(local, mesh=mesh, in_specs=in_specs, out_specs=out_specs, check_vma=False)
```

profile of v0, /device:TPU:17, one launch (start us, length us, event | category | flops | bytes accessed | tf_op | source)
XLA Modules:
  0.0 331.0 jit_solution(5679777323317801051)
XLA Ops:
  6.5 0.0 copy-start
  6.5 0.0 all-gather.2.cloned.1.call-start
  6.5 0.7 all-gather.2.cloned.1.call-update
  7.3 0.0 reduce-scatter.2.cloned.1.call-start
  7.4 124.7 %all-gather.2.cloned.1.call-done = bf16[2048,4096]{1,0:T(8,128)(2,1)} async-done(((bf16[2048,256]{1,0:T(8,128)(2,1)}), bf16[2048,4096]{1,0:T(8,128)(2,1)}) %all-gather.2.cloned.1.call-update) | async-done | bytes 16777232 | tf_op jit(solution)/shard_map/all_gather | solution.py:35
  132.0 11.1 %convolution_convert_fusion.2 = bf16[2048,256]{1,0:T(8,128)(2,1)S(1)} fusion(bf16[2048,4096]{1,0:T(8,128)(2,1)} %all-gather.2.cloned.1.call-done, bf16[4096,256]{1,0:T(8,128)(2,1)} %param.10), kind=kOutput, calls=%fused_computation.4 | convolution fusion | flops 4295491584 | bytes 19922944 | tf_op jit(solution)/shard_map/dot_general | solution.py:38
  143.1 1.3 reshape.28
  144.4 2.4 copy.23
  146.8 12.0 %convolution_convert_fusion.3 = bf16[2048,256]{1,0:T(8,128)(2,1)} fusion(bf16[2048,4096]{1,0:T(8,128)(2,1)} %all-gather.2.cloned.1.call-done, bf16[4096,256]{1,0:T(8,128)(2,1)} %param.9), kind=kOutput, calls=%fused_computation.5 | convolution fusion | flops 4295491584 | bytes 19922944 | tf_op jit(solution)/shard_map/dot_general | solution.py:38
  158.8 2.1 reshape.27
  160.9 1.7 fusion.2
  162.6 0.0 copy-start.1
  162.6 1.1 fusion.12
  163.7 1.1 slice.10
  164.8 0.0 copy-done.1
  164.8 9.2 %convolution_convert_fusion.1 = bf16[2048,256]{1,0:T(8,128)(2,1)} fusion(bf16[2048,4096]{1,0:T(8,128)(2,1)} %all-gather.2.cloned.1.call-done, bf16[4096,256]{1,0:T(8,128)(2,1)S(1)} %copy-done.1), kind=kOutput, calls=%fused_computation.3 | convolution fusion | flops 4295491584 | bytes 19922944 | tf_op jit(solution)/shard_map/dot_general | solution.py:38
  174.0 2.2 reshape.29
  176.2 14.3 %all_gather.8 = bf16[8,2,128,128]{3,2,1,0:T(8,128)(2,1)} all-gather(bf16[1,2,128,128]{3,2,1,0:T(8,128)(2,1)S(1)} %slice.12), channel_id=1, replica_groups=mesh['seq'=8,'tensor'=16] {'seq'}, dimensions={0}, use_global_device_ids=true | all-gather | bytes 589824 | tf_op jit(solution)/shard_map/all_gather | solution.py:14
  190.5 7.4 %while.14 = (s32[]{:T(128)}, f32[2,128,128]{2,1,0:T(8,128)S(1)}, s32[]{:T(128)}, bf16[8,2,128,128]{3,2,1,0:T(8,128)(2,1)}, s32[]{:T(128)}, /*index=5*/s32[]{:T(128)}) while((s32[]{:T(128)}, f32[2,128,128]{2,1,0:T(8,128)S(1)}, s32[]{:T(128)}, bf16[8,2,128,128]{3,2,1,0:T(8,128)(2,1)}, s32[]{:T(128)}, /*index=5*/s32[]{:T(128)}) %tuple.32), condition=%wide.region_2.3_spmd.clone, body=%wide.region_1.2_spmd.clone.sunk | while | flops 131076 | bytes 327773 | solution.py:22
  190.6 0.9 add_select_fusion.2
  191.5 0.9 add_select_fusion.2
  192.4 0.9 add_select_fusion.2
  193.3 0.9 add_select_fusion.2
  194.3 0.9 add_select_fusion.2
  195.2 0.9 add_select_fusion.2
  196.1 0.9 add_select_fusion.2
  197.0 0.9 add_select_fusion.2
  198.0 4.2 %fusion = f32[8,2,128,256]{3,2,1,0:T(8,128)} fusion(bf16[8,256,2,128]{1,3,2,0:T(8,128)(2,1)S(1)} %copy.23, pred[256,256]{1,0:T(8,128)(4,1)S(1)} %iota_compare_fusion, bf16[8,256,2,128]{3,2,1,0:T(2,128)(2,1)} %reshape.27, bf16[8,256,2,128]{3,2,1,0:T(2,128)(2,1)} %reshape.29), kind=kOutput, calls=%fused_computation.7 | convolution fusion | flops 538968064 | bytes 5308416 | tf_op jit(solution)/shard_map/nhbc,nche->nbhe/dot_general | solution.py:60
  202.2 2.7 fusion.1
  204.9 0.6 copy.24
  205.5 0.3 copy.26
  205.8 0.0 copy-done
  205.8 8.1 %convolution_convert_fusion = bf16[2048,4096]{1,0:T(8,128)(2,1)} fusion(bf16[2048,256]{0,1:T(8,128)(2,1)S(1)} %bitcast.23, bf16[256,4096]{1,0:T(8,128)(2,1)S(1)} %copy-done), kind=kOutput, calls=%fused_computation.1 | convolution fusion | flops 4303355904 | bytes 19922944 | tf_op jit(solution)/shard_map/dot_general | solution.py:62
  213.9 0.0 reduce-scatter.2.cloned.1.call-update
  213.9 110.2 %reduce-scatter.2.cloned.1.call-done = bf16[2048,256]{1,0:T(8,128)(2,1)} async-done(((bf16[2048,4096]{1,0:T(8,128)(2,1)}), bf16[2048,256]{1,0:T(8,128)(2,1)}) %reduce-scatter.2.cloned.1.call-update) | async-done | bytes 1048592 | tf_op jit(solution)/shard_map/reduce_scatter | solution.py:63
  (3 shorter events, 0.0 us)
Async XLA Ops:
  6.5 199.2 %copy-start = (bf16[256,4096]{1,0:T(8,128)(2,1)S(1)}, bf16[256,4096]{1,0:T(8,128)(2,1)}, u32[]{:S(2)}) copy-start(bf16[256,4096]{1,0:T(8,128)(2,1)} %param.11) | copy-start | bytes 6291460
  6.5 125.5 %all-gather.2.cloned.1.call-start = ((), (), s32[]{:S(2)}) async-start(), calls=%async_computation.1 | async-start | bytes 17825792 | tf_op jit(solution)/shard_map/all_gather | solution.py:35
  7.3 316.9 %reduce-scatter.2.cloned.1.call-start = ((), (), s32[]{:S(2)}) async-start(), calls=%async_computation.2 | async-start | bytes 17825792 | tf_op jit(solution)/shard_map/reduce_scatter | solution.py:63
  162.6 2.2 copy-start.1
Sparse Core Ops, SparseCore 0:
  9.5 122.4 all-gather.1
  214.0 110.0 reduce-scatter.1
where the time goes:
time: 333 us; the launch traced here: 331 us
  waiting for transfers between devices  236 us (71%)
  matrix products  49 us (15%)
  blocking collectives  14.3 us (4%)
  between operations  13.5 us (4%)
  local copies, waits for them, and re-layouts  9.95 us (3%)
  other arithmetic  8.35 us (3%)
    all_gather x1, waiting for transfers between devices, local(): shard_piece = lax.all_gather(tokens, 'tensor', axis=1, tiled=True)  125 us
    reduce_scatter x1, waiting for transfers between devices, local(): lax.psum_scatter(partial_out.astype(jnp.bfloat16), 'tensor', scatter_dime...  110 us
    dot_general x3, matrix products, local(): jnp.dot(shard_piece, weight, preferred_element_type=jnp.float32)  32.3 us
    all_gather x1, blocking collectives, carried_in(): everything = lax.all_gather(array.astype(jnp.bfloat16), axis)  14.3 us
    dot_general x1, matrix products, local(): jnp.dot(attended, w_output, preferred_element_type=jnp.float32)  8.11 us
    select_n x8, other arithmetic, step(): return jnp.where(reached, new, before)  7.23 us
  transfers between devices with their start and end apart: 2, of which 2 were waited for; matrix products, arithmetic and copies ran while one was open for 0% of the time, Pallas kernels for 0%

commit v1 on v0

v1 whole, which is shorter than its diff:
```python
import math

import jax
import jax.numpy as jnp
from jax import lax
from jax.experimental import pallas as pl
from jax.experimental.pallas import tpu as pltpu
from jax.sharding import PartitionSpec as P

DH = 128
BLOCK = 256
BF = jnp.bfloat16
F32 = jnp.float32
NB = 8
RX = 160
RZ = BLOCK - RX
HZ = RZ // 2
OC = 128
NO = 8
FEAT = 256
SIB = 15
SIB3 = 7


def remote(src, dst, send, recv, device):
    return pltpu.make_async_remote_copy(
        src_ref=src, dst_ref=dst, send_sem=send, recv_sem=recv,
        device_id=device, device_id_type=pl.DeviceIdType.MESH,
    )


def kernel(scale, tok, wq, wk, wv, wo, out,
           xg, w, q, qkv, intra, st, run, tot, carry, low, attn, ag, wog, outb,
           pre_s, pre_r, w_l, w1_s, w1_r, w2_s, w2_r, o1_s, o1_r, o2_s, o2_r, o3_s, o3_r,
           g_s, g_r, t_s, t_r, a_s, a_r, r_s, r_r):
    div, rem = lax.div, lax.rem
    seq, ten = lax.axis_index("seq"), lax.axis_index("tensor")
    y, c, x, z = div(seq, 2), rem(seq, 2), div(ten, 4), rem(ten, 4)
    half, xi = div(x, 2), rem(x, 2)
    xn, xc = x + 1 - 2 * xi, 3 - x
    mine = c == half
    other = jnp.logical_not(mine)
    shard = 2 * y + half
    zp, zm, z2 = rem(z + 1, 4), rem(z + 3, 4), rem(z + 2, 4)

    def at(y_, c_, x_, z_):
        return (2 * y_ + c_, 4 * x_ + z_)

    d_xn, d_zp, d_zm = at(y, c, xn, z), at(y, c, x, zp), at(y, c, x, zm)
    d_sib, d_part = at(y, 1 - c, x, z), at(y, 1 - c, xc, z)

    def col(x_, z_, own=True):
        natural = mine if own else other
        return pl.multiple_of((jnp.where(natural, x_, 3 - x_) * 4 + z_) * FEAT, FEAT)

    places = ((x, z), (xn, z), (x, zm), (x, zp), (xn, zm), (xn, zp), (x, z2), (xn, z2))
    cols = [col(*p) for p in places]
    sib_cols = [col(*p, own=False) for p in places]
    c_own, c_x, c_m, c_p, c_xm, c_xp, c_2, c_x2 = cols

    barrier = pltpu.get_barrier_semaphore()
    peers = [d_sib, d_part, at(y, 1 - c, xc + 1 - 2 * rem(xc, 2), z)]
    for d in (1, 2, 3):
        peers += [at(y, c, x, rem(z + d, 4)), at(y, c, rem(x + d, 4), z),
                  at(rem(y + d, 4), c, x, z), at(rem(y + d, 4), c, xc, z)]
    for peer in peers:
        pl.semaphore_signal(barrier, inc=1, device_id=peer, device_id_type=pl.DeviceIdType.MESH)
    pl.semaphore_wait(barrier, len(peers))

    t_col = pl.multiple_of(ten * FEAT, FEAT)
    p_col = pl.multiple_of((4 * xc + z) * FEAT, FEAT)
    w_hbm = (wq, wk, wv)
    quarter = pl.ds(pl.multiple_of(y * 1024, 1024), 1024)

    def block_rows(r):
        return pl.ds(pl.multiple_of(r * BLOCK, BLOCK), BLOCK)

    def tok_local(r):
        return pltpu.make_async_copy(tok.at[block_rows(r)], xg.at[r, :, pl.ds(t_col, FEAT)], pre_r.at[r])

    def tok_remote(r):
        return remote(tok.at[block_rows(r)], xg.at[r, :, pl.ds(t_col, FEAT)], pre_s.at[r], pre_r.at[r], d_part)

    def tok_wait(r):
        slot = xg.at[r, :, pl.ds(c_own, FEAT)]
        pltpu.make_async_copy(tok.at[block_rows(r)], slot, pre_r.at[r]).wait()

    def w_local(n):
        return pltpu.make_async_copy(w_hbm[n], w.at[n], w_l.at[n])

    def w_first(n):
        return remote(w_hbm[n].at[quarter], w.at[n, quarter], w1_s.at[n], w1_r.at[n], d_part)

    def w_second(n, d):
        return remote(w.at[n, quarter], w.at[n, quarter], w2_s.at[n, d], w2_r.at[n, d],
                      at(rem(y + d, 4), c, x, z))

    o_cols = pl.ds(pl.multiple_of(rem(y, 2) * DH, DH), DH)
    o_blk = div(y, 2)

    def o_source(z_):
        return wo.at[:, pl.ds(pl.multiple_of(((2 * c + o_blk) * 4 + z_) * FEAT + rem(y, 2) * DH, DH), DH)]

    o_mine = wog.at[o_blk, pl.ds(pl.multiple_of(ten * FEAT, FEAT), FEAT), o_cols]

    def o_first(d):
        if d == 0:
            return pltpu.make_async_copy(o_source(z), o_mine, o1_r.at[0])
        to = rem(z + d, 4)
        return remote(o_source(to), o_mine, o1_s.at[d], o1_r.at[d], at(y, c, x, to))

    def o_second(d):
        part = wog.at[o_blk, pl.ds(pl.multiple_of(x * 1024, 1024), 1024), o_cols]
        return remote(part, part, o2_s.at[d], o2_r.at[d], at(y, c, rem(x + d, 4), z))

    def o_third(d):
        part = wog.at[o_blk, :, o_cols]
        return remote(part, part, o3_s.at[d], o3_r.at[d], at(rem(y + d, 4), c, x, z))

    @pl.when(mine)
    def _():
        def start(r, _):
            tok_local(r).start()
            return 0
        lax.fori_loop(0, NB, start, 0)
        for n in range(3):
            w_local(n).start()

    def send_inputs(k):
        for step in range(4):
            @pl.when(jnp.logical_and(other, k == step))
            def _(step=step):
                tok_remote(2 * step).start()
                tok_remote(2 * step + 1).start()
                if step < 3:
                    w_first(step).start()
        for step in range(3):
            @pl.when(jnp.logical_and(other, k == step + 2))
            def _(step=step):
                w_first(step).wait_recv()
                for d in (1, 2, 3):
                    w_second(step, d).start()

        @pl.when(k == 1)
        def _():
            for d in range(4):
                o_first(d).start()

        @pl.when(k == 4)
        def _():
            o_first(0).wait()
            for d in (1, 2, 3):
                o_first(d).wait_recv()
            for d in (1, 2, 3):
                o_second(d).start()

        @pl.when(k == 7)
        def _():
            for d in (1, 2, 3):
                o_second(d).wait_recv()
            for d in (1, 2, 3):
                o_third(d).start()

    ALL, XF, ZF = pl.ds(0, BLOCK), pl.ds(0, RX), pl.ds(RX, RZ)
    Z1, Z2 = pl.ds(RX, HZ), pl.ds(RX + HZ, HZ)

    def gather(r, k, rows, column, device=None):
        slot = xg.at[r, rows, pl.ds(column, FEAT)]
        return remote(slot, slot, g_s.at[r, k], g_r.at[r, k], d_sib if device is None else device)

    def to_sibling(r, piece):
        gather(r, SIB + piece, ALL, cols[piece]).start()

    def hop0(r):
        tok_wait(r)
        gather(r, 0, XF, c_own, d_xn).start()
        gather(r, 8, ZF, c_own, d_zp).start()
        gather(r, 9, ZF, c_own, d_zm).start()
        gather(r, 1, XF, c_own, d_zp).start()
        gather(r, 2, XF, c_own, d_zm).start()
        gather(r, 7, ZF, c_own, d_xn).start()
        to_sibling(r, 0)

    def hop1(r):
        gather(r, 0, XF, c_x).wait_recv()
        gather(r, 3, XF, c_x, d_zp).start()
        gather(r, 4, XF, c_x, d_zm).start()
        gather(r, 8, ZF, c_m).wait_recv()
        gather(r, 10, Z1, c_m, d_zp).start()
        gather(r, 12, ZF, c_m, d_xn).start()
        gather(r, 9, ZF, c_p).wait_recv()
        gather(r, 11, Z2, c_p, d_zm).start()
        gather(r, 13, ZF, c_p, d_xn).start()
        gather(r, 1, XF, c_m).wait_recv()
        gather(r, 5, XF, c_m, d_zp).start()
        to_sibling(r, 2)
        gather(r, 2, XF, c_p).wait_recv()
        to_sibling(r, 3)
        gather(r, 7, ZF, c_x).wait_recv()
        to_sibling(r, 1)

    def hop2(r):
        gather(r, 4, XF, c_xp).wait_recv()
        gather(r, 6, XF, c_xp, d_zm).start()
        gather(r, 10, Z1, c_2).wait_recv()
        gather(r, 11, Z2, c_2).wait_recv()
        gather(r, 14, ZF, c_2, d_xn).start()
        gather(r, 3, XF, c_xm).wait_recv()
        gather(r, 12, ZF, c_xm).wait_recv()
        to_sibling(r, 4)
        gather(r, 13, ZF, c_xp).wait_recv()
        to_sibling(r, 5)

    def hop3(r):
        gather(r, 5, XF, c_2).wait_recv()
        to_sibling(r, 6)
        gather(r, 6, XF, c_x2).wait_recv()
        gather(r, 14, ZF, c_x2).wait_recv()
        to_sibling(r, 7)

    def heads(n):
        return slice(n * DH, (n + 1) * DH)

    def state_copy(to):
        to_y, to_half = div(to, 2), rem(to, 2)
        to_x = jnp.where(to_half == half, x, xc)
        return remote(tot, carry.at[shard], t_s.at[to], t_r.at[shard], at(to_y, c, to_x, z))

    def block(r, _):
        for piece in range(8):
            gather(r, SIB + piece, ALL, sib_cols[piece]).wait_recv()

        def project(n, _):
            qkv[n] = jnp.dot(xg[r], w[n], preferred_element_type=F32).astype(BF)
            return 0
        lax.fori_loop(0, 3, project, 0)
        q[r] = qkv[0]
        for n in range(2):
            total = run[n]
            st[r, n] = total
            run[n] = total + lax.dot_general(
                qkv[1, :, heads(n)], qkv[2, :, heads(n)], (((0,), (0,)), ((), ())), preferred_element_type=F32)

        @pl.when(r == NB - 1)
        def _():
            tot[...] = run[...].astype(BF)

            def send(to, _):
                state_copy(to).start()
                return 0
            lax.fori_loop(shard + 1, 8, send, 0)

        causal = (lax.broadcasted_iota(jnp.int32, (BLOCK, BLOCK), 0)
                  >= lax.broadcasted_iota(jnp.int32, (BLOCK, BLOCK), 1))
        for n in range(2):
            scores = lax.dot_general(
                qkv[0, :, heads(n)], qkv[1, :, heads(n)], (((1,), (1,)), ((), ())), preferred_element_type=F32)
            scores = jnp.where(causal, scores, 0.0).astype(BF)
            intra[r, :, heads(n)] = jnp.dot(scores, qkv[2, :, heads(n)], preferred_element_type=F32)
        return 0

    run[...] = jnp.zeros_like(run)

    def round1(k, _):
        send_inputs(k)

        @pl.when(k < NB)
        def _():
            hop0(k)

        @pl.when(jnp.logical_and(k >= 1, k < NB + 1))
        def _():
            hop1(k - 1)

        @pl.when(jnp.logical_and(k >= 2, k < NB + 2))
        def _():
            hop2(k - 2)

        @pl.when(jnp.logical_and(k >= 3, k < NB + 3))
        def _():
            hop3(k - 3)

        @pl.when(jnp.logical_and(mine, k == 6))
        def _():
            for n in range(3):
                w_local(n).wait()

        @pl.when(jnp.logical_and(other, k == 6))
        def _():
            for n in range(3):
                for d in (1, 2, 3):
                    w_second(n, d).wait_recv()

        def done(k_):
            return jnp.maximum(jnp.minimum(k_ - 2, 2 * (k_ - 5)), 0)
        lax.fori_loop(done(k - 1), done(k), block, 0)
        return 0
    lax.fori_loop(0, NB + 3, round1, 0)

    run[...] = jnp.zeros_like(run)

    def add(k, _):
        remote(tot, carry.at[k], t_s.at[k], t_r.at[k], d_sib).wait_recv()
        run[...] += carry[k].astype(F32)
        return 0
    lax.fori_loop(0, shard, add, 0)

    def lower(r, _):
        low[r] = (st[r] + run[...]).astype(BF)
        return 0
    lax.fori_loop(0, NB, lower, 0)

    def attended(r, sub):
        rows = pl.ds(pl.multiple_of(sub * OC, OC), OC)
        parts = []
        for n in range(2):
            inter = jnp.dot(q[r, rows, heads(n)], low[r, n], preferred_element_type=F32)
            parts.append(((inter + intra[r, rows, heads(n)]) * scale).astype(BF))
        return jnp.concatenate(parts, axis=1)

    def spread(m, k, column, device=None):
        slot = ag.at[m, :, pl.ds(column, FEAT)]
        return remote(slot, slot, a_s.at[m, k], a_r.at[m, k], d_sib if device is None else device)

    def spread_sibling(m, piece):
        spread(m, SIB3 + piece, cols[piece]).start()

    def hand_over(m):
        return remote(attn.at[m], ag.at[m, :, pl.ds(c_own, FEAT)], a_s.at[m, 0], a_r.at[m, 0], d_xn)

    def turn0(m):
        r, sub = 2 * div(m, 2), rem(m, 2)
        ag[m, :, pl.ds(c_own, FEAT)] = attended(r + xi, sub)
        spread(m, 1, c_own, d_zp).start()
        spread(m, 2, c_own, d_zm).start()
        attn[m] = attended(r + 1 - xi, sub)
        hand_over(m).start()
        spread_sibling(m, 0)

    def turn1(m):
        spread(m, 0, c_x).wait_recv()
        spread(m, 3, c_x, d_zp).start()
        spread(m, 4, c_x, d_zm).start()
        spread_sibling(m, 1)
        spread(m, 1, c_m).wait_recv()
        spread(m, 5, c_m, d_zp).start()
        spread_sibling(m, 2)
        spread(m, 2, c_p).wait_recv()
        spread_sibling(m, 3)

    def turn2(m):
        spread(m, 4, c_xp).wait_recv()
        spread(m, 6, c_xp, d_zm).start()
        spread_sibling(m, 5)
        spread(m, 3, c_xm).wait_recv()
        spread_sibling(m, 4)

    def turn3(m):
        spread(m, 5, c_2).wait_recv()
        spread_sibling(m, 6)
        spread(m, 6, c_x2).wait_recv()
        spread_sibling(m, 7)

    def out_rows(m):
        return pl.ds(pl.multiple_of((2 * div(m, 2) + xi) * BLOCK + rem(m, 2) * OC, OC), OC)

    def out_chunk(m):
        return 2 * (2 * div(m, 2) + xi) + rem(m, 2)

    def result(m, n):
        return remote(outb.at[m, n], out.at[out_rows(m)], r_s.at[m, n], r_r.at[out_chunk(m)],
                      at(y, half, 2 * c + n, z))

    def result_local(m, n):
        return pltpu.make_async_copy(outb.at[m, n], out.at[out_rows(m)], r_r.at[out_chunk(m)])

    def turn4(m):
        for piece in range(8):
            spread(m, SIB3 + piece, sib_cols[piece]).wait_recv()

        def multiply(n, _):
            outb[m, n] = jnp.dot(ag[m], wog[n], preferred_element_type=F32).astype(BF)
            here = jnp.logical_and(mine, n == xi)

            @pl.when(here)
            def _():
                result_local(m, n).start()

            @pl.when(jnp.logical_not(here))
            def _():
                result(m, n).start()
            return 0
        lax.fori_loop(0, 2, multiply, 0)

    def round3(k, _):
        @pl.when(k < NO)
        def _():
            turn0(k)

        @pl.when(jnp.logical_and(k >= 1, k < NO + 1))
        def _():
            turn1(k - 1)

        @pl.when(jnp.logical_and(k >= 2, k < NO + 2))
        def _():
            turn2(k - 2)

        @pl.when(jnp.logical_and(k >= 3, k < NO + 3))
        def _():
            turn3(k - 3)

        @pl.when(k == 4)
        def _():
            for d in (1, 2, 3):
                o_third(d).wait_recv()

        @pl.when(k >= 4)
        def _():
            turn4(k - 4)
        return 0
    lax.fori_loop(0, NO + 4, round3, 0)

    g_rows = [XF] * 7 + [ZF] * 3 + [Z1, Z2] + [ZF] * 3 + [ALL] * 8

    def sent1(r, _):
        for k, rows in enumerate(g_rows):
            gather(r, k, rows, c_own).wait_send()
        return 0
    lax.fori_loop(0, NB, sent1, 0)

    def sent3(m, _):
        for k in range(15):
            spread(m, k, c_own).wait_send()
        for n in range(2):
            @pl.when(jnp.logical_not(jnp.logical_and(mine, n == xi)))
            def _(n=n):
                result(m, n).wait_send()
        return 0
    lax.fori_loop(0, NO, sent3, 0)

    @pl.when(other)
    def _():
        for r in range(NB):
            tok_remote(r).wait_send()
        for n in range(3):
            w_first(n).wait_send()
            for d in (1, 2, 3):
                w_second(n, d).wait_send()
    for d in (1, 2, 3):
        o_first(d).wait_send()
        o_second(d).wait_send()
        o_third(d).wait_send()

    def sent_state(to, _):
        state_copy(to).wait_send()
        return 0
    lax.fori_loop(shard + 1, 8, sent_state, 0)

    def landed(k, _):
        rows = pl.ds(pl.multiple_of(k * OC, OC), OC)
        pltpu.make_async_copy(outb.at[0, 0], out.at[rows], r_r.at[k]).wait()
        return 0
    lax.fori_loop(0, 16, landed, 0)


def local(scale, tokens, w_query, w_key, w_value, w_output):
    rows, feat = tokens.shape
    wide = w_query.shape[0]
    dma, vmem = pltpu.SemaphoreType.DMA, pltpu.VMEM
    return pl.pallas_call(
        lambda *refs: kernel(scale, *refs),
        out_shape=jax.ShapeDtypeStruct((rows, feat), BF),
        in_specs=[pl.BlockSpec(memory_space=pl.ANY)] * 5,
        out_specs=pl.BlockSpec(memory_space=pl.ANY),
        scratch_shapes=[
            vmem((NB, BLOCK, wide), BF),
            vmem((3, wide, FEAT), BF),
            vmem((NB, BLOCK, FEAT), BF),
            vmem((3, BLOCK, FEAT), BF),
            vmem((NB, BLOCK, FEAT), F32),
            vmem((NB, 2, DH, DH), F32),
            vmem((2, DH, DH), F32),
            vmem((2, DH, DH), BF),
            vmem((8, 2, DH, DH), BF),
            vmem((NB, 2, DH, DH), BF),
            vmem((NO, OC, FEAT), BF),
            vmem((NO, OC, wide), BF),
            vmem((2, wide, FEAT), BF),
            vmem((NO, 2, OC, FEAT), BF),
            dma((NB,)), dma((NB,)),
            dma((3,)),
            dma((3,)), dma((3,)),
            dma((3, 4)), dma((3, 4)),
            dma((4,)), dma((4,)),
            dma((4,)), dma((4,)),
            dma((4,)), dma((4,)),
            dma((NB, 23)), dma((NB, 23)),
            dma((8,)), dma((8,)),
            dma((NO, 15)), dma((NO, 15)),
            dma((NO, 2)), dma((16,)),
        ],
        name="layer",
        cost_estimate=pl.CostEstimate(flops=18_000_000_000, bytes_accessed=12 << 20, transcendentals=0),
        compiler_params=pltpu.CompilerParams(
            collective_id=0, has_side_effects=True, vmem_limit_bytes=56 << 20),
    )(tokens, w_query, w_key, w_value, w_output)


def solution(mesh):
    scale = 1.0 / math.sqrt(DH * 16384)
    in_specs = (
        P("seq", "tensor"),
        P(None, "tensor"),
        P(None, "tensor"),
        P(None, "tensor"),
        P("tensor", None),
    )
    return jax.shard_map(
        lambda *args: local(scale, *args),
        mesh=mesh, in_specs=in_specs, out_specs=P("seq", "tensor"), check_vma=False)
```

time: 333 us -> 161 us (0.48)
  waiting for transfers between devices: 236 us -> 0 us
  Pallas kernels: 0 us -> 159 us
  matrix products: 49 us -> 0 us
  blocking collectives: 14.3 us -> 0 us
  between operations: 13.5 us -> 0.01 us
  other arithmetic: 8.35 us -> 0 us
  local copies, waits for them, and re-layouts: 9.95 us -> 2.26 us
    pallas_call x0 -> x1, Pallas kernels: none -> 159 us  [local(): pl.pallas_call(lambda *refs: kernel(scale, *refs), out_shape=jax.ShapeDty...]
    all_gather x1 -> x0, waiting for transfers between devices: 125 us -> none  [local(): shard_piece = lax.all_gather(tokens, 'tensor', axis=1, tiled=True)]
    reduce_scatter x1 -> x0, waiting for transfers between devices: 110 us -> none  [local(): lax.psum_scatter(partial_out.astype(jnp.bfloat16), 'tensor', scatter_dime...]
    dot_general x7 -> x0, matrix products: 49 us -> none  [the longest x3 32.3 us: local(): jnp.dot(shard_piece, weight, preferred_element_type=jnp.float32)]
    all_gather x1 -> x0, blocking collectives: 14.3 us -> none  [carried_in(): everything = lax.all_gather(array.astype(jnp.bfloat16), axis)]
    reshape x4 -> x0, local copies, waits for them, and re-layouts: 7.98 us -> none  [the longest x2 3.68 us: local(): value_all = value_sum.astype(jnp.bfloat16).reshape(shape_blocks)]
    select_n x8 -> x0, other arithmetic: 7.23 us -> none  [step(): return jnp.where(reached, new, before)]
  transfers between devices with their start and end apart: 2 -> 0, of which waited for: 2 -> 0; matrix products, arithmetic and copies ran while one was open for 0% -> 0% of each run, Pallas kernels for 0% -> 0%
where the time goes in v1:
time: 161 us
  Pallas kernels  159 us (99%)
  local copies, waits for them, and re-layouts  2.26 us (1%)
    pallas_call x1, Pallas kernels, local(): pl.pallas_call(lambda *refs: kernel(scale, *refs), out_shape=jax.ShapeDty...  159 us

profile of v1, /device:TPU:17, one launch (start us, length us, event | category | flops | bytes accessed | tf_op | source)
XLA Modules:
  0.0 161.1 jit_solution(16523526326287985323)
XLA Ops:
  0.0 158.8 %layer.1 = bf16[2048,256]{1,0:T(8,128)(2,1)} custom-call(bf16[2048,256]{1,0:T(8,128)(2,1)} %refs_0_.1, bf16[4096,256]{1,0:T(8,128)(2,1)} %refs_1_.1, bf16[4096,256]{1,0:T(8,128)(2,1)} %refs_2_.1, bf16[4096,256]{1,0:T(8,128)(2,1)} %refs_3_.1, bf16[256,4096]{1,0:T(8,128)(2,1)} %refs_4_.1), custom_call_target="tpu_custom_call" | custom-call | flops 17999998976 | bytes 12582912 | tf_op jit(solution)/shard_map/layer/pallas_call | solution.py:470
  158.8 2.3 %copy.7 = bf16[2048,256]{1,0:T(8,128)(2,1)} copy(bf16[2048,256]{1,0:T(8,128)(2,1)} %layer.1) | data formatting | bytes 2097152

commit v2 on v1

v2 whole, which is shorter than its diff:
```python
import math

import jax
import jax.numpy as jnp
from jax import lax
from jax.experimental import pallas as pl
from jax.experimental.pallas import tpu as pltpu
from jax.sharding import PartitionSpec as P

DH = 128
BLOCK = 256
BF = jnp.bfloat16
F32 = jnp.float32
NB = 8
CH = 128
NC = 16
RX = 80
RZ = CH - RX
HZ = 32
OC = 128
NO = 8
FEAT = 256
SIB = 15
SIB3 = 7
AHEAD = 1
LATE = 12
AHEAD3 = 1


def remote(src, dst, send, recv, device):
    return pltpu.make_async_remote_copy(
        src_ref=src, dst_ref=dst, send_sem=send, recv_sem=recv,
        device_id=device, device_id_type=pl.DeviceIdType.MESH,
    )


def wide_rows(gathered, index):
    return jnp.concatenate([gathered[index, p] for p in range(16)], axis=1)


def kernel(scale, tok, wq, wk, wv, wo, out,
           xg, w, q, qkv, intra, st, run, tot, carry, low, attn, ag, wog, outb,
           pre_s, pre_r, w_l, w1_s, w1_r, w2_s, w2_r, o1_s, o1_r, o2_s, o2_r, o3_s, o3_r,
           g_s, g_r, t_s, t_r, a_s, a_r, r_s, r_r):
    div, rem = lax.div, lax.rem
    seq, ten = lax.axis_index("seq"), lax.axis_index("tensor")
    y, c, x, z = div(seq, 2), rem(seq, 2), div(ten, 4), rem(ten, 4)
    half, xi = div(x, 2), rem(x, 2)
    xn, xc = x + 1 - 2 * xi, 3 - x
    xd = 3 - xn
    mine = c == half
    other = jnp.logical_not(mine)
    shard = 2 * y + half
    zp, zm, z2 = rem(z + 1, 4), rem(z + 3, 4), rem(z + 2, 4)

    def at(y_, c_, x_, z_):
        return (2 * y_ + c_, 4 * x_ + z_)

    d_xn, d_zp, d_zm = at(y, c, xn, z), at(y, c, x, zp), at(y, c, x, zm)
    d_sib, d_part = at(y, 1 - c, x, z), at(y, 1 - c, xc, z)

    def col(x_, z_):
        return jnp.where(mine, x_, 3 - x_) * 4 + z_

    places = ((x, z), (xn, z), (x, zm), (x, zp), (xn, zm), (xn, zp), (x, z2), (xn, z2))
    cols = [col(*p) for p in places]
    c_own, c_x, c_m, c_p, c_xm, c_xp, c_2, c_x2 = cols

    barrier = pltpu.get_barrier_semaphore()
    peers = [d_sib, d_part, at(y, 1 - c, xd, z)]
    for d in (1, 2, 3):
        peers += [at(y, c, x, rem(z + d, 4)), at(y, c, rem(x + d, 4), z),
                  at(rem(y + d, 4), c, x, z), at(rem(y + d, 4), c, xc, z)]
    for peer in peers:
        pl.semaphore_signal(barrier, inc=1, device_id=peer, device_id_type=pl.DeviceIdType.MESH)
    pl.semaphore_wait(barrier, len(peers))

    w_hbm = (wq, wk, wv)
    quarter = pl.ds(pl.multiple_of(y * 1024, 1024), 1024)

    def tok_rows(r):
        return tok.at[pl.ds(pl.multiple_of(r * CH, CH), CH)]

    def slot(r, piece, first=0, count=CH):
        rows = pl.ds(pl.multiple_of(rem(r, 2) * CH + first, 16), count)
        return xg.at[div(r, 2), piece, rows]

    def tok_local(r):
        return pltpu.make_async_copy(tok_rows(r), slot(r, ten), pre_r.at[r])

    def tok_remote(r):
        return remote(tok_rows(r), slot(r, ten), pre_s.at[r], pre_r.at[r], d_part)

    def tok_wait(r):
        pltpu.make_async_copy(tok_rows(r), slot(r, c_own), pre_r.at[r]).wait()

    def w_local(n):
        return pltpu.make_async_copy(w_hbm[n], w.at[n], w_l.at[n])

    def w_first(n):
        return remote(w_hbm[n].at[quarter], w.at[n, quarter], w1_s.at[n], w1_r.at[n], d_part)

    yp, ym, y2 = rem(y + 1, 4), rem(y + 3, 4), rem(y + 2, 4)
    d_yp, d_ym = at(yp, c, x, z), at(ym, c, x, z)

    def w_copy(n, k, y_, first, count, device=None):
        rows = pl.ds(pl.multiple_of(y_ * 1024 + first, 16), count)
        return remote(w.at[n, rows], w.at[n, rows], w2_s.at[n, k], w2_r.at[n, k], d_yp if device is None else device)

    def w_second(n):
        return [w_copy(n, 0, y, 0, 1024, d_yp), w_copy(n, 1, y, 0, 1024, d_ym)]

    def w_second_in(n):
        return [w_copy(n, 0, ym, 0, 1024), w_copy(n, 1, yp, 0, 1024)]

    def w_third(n):
        return [w_copy(n, 2, ym, 0, 512, d_yp), w_copy(n, 3, yp, 512, 512, d_ym)]

    def w_third_in(n):
        return [w_copy(n, 2, y2, 0, 512), w_copy(n, 3, y2, 512, 512)]

    o_cols = pl.ds(pl.multiple_of(rem(y, 2) * DH, DH), DH)
    o_blk = div(y, 2)

    def o_source(z_):
        return wo.at[:, pl.ds(pl.multiple_of(((2 * c + o_blk) * 4 + z_) * FEAT + rem(y, 2) * DH, DH), DH)]

    o_mine = wog.at[o_blk, pl.ds(pl.multiple_of(ten * FEAT, FEAT), FEAT), o_cols]

    def o_first(d):
        if d == 0:
            return pltpu.make_async_copy(o_source(z), o_mine, o1_r.at[0])
        to = rem(z + d, 4)
        return remote(o_source(to), o_mine, o1_s.at[d], o1_r.at[d], at(y, c, x, to))

    def o_part(k, x_, to, first=0, count=1024):
        rows = pl.ds(pl.multiple_of(x_ * 1024 + first, 16), count)
        part = wog.at[o_blk, rows, o_cols]
        place = div(first, 128) if k == 0 and count < 1024 else 8
        return remote(part, part, o2_s.at[k], o2_r.at[k, place], at(y, c, to, z))

    def o_copy(k, y_, first, count, device=None):
        rows, columns = pl.ds(pl.multiple_of(first, 16), count), pl.ds(pl.multiple_of(rem(y_, 2) * DH, DH), DH)
        part = wog.at[div(y_, 2), rows, columns]
        return remote(part, part, o3_s.at[k], o3_r.at[k], d_yp if device is None else device)

    def o_third(x_):
        return [o_copy(0, y, x_ * 1024, 1024, d_yp), o_copy(1, y, x_ * 1024, 1024, d_ym)]

    def o_third_out():
        return [o_copy(0, y, 0, 4096, d_yp), o_copy(1, y, 0, 4096, d_ym)]

    def o_third_in():
        return [o_copy(0, ym, 0, 4096), o_copy(1, yp, 0, 4096)]

    def o_fourth():
        return [o_copy(2, ym, 0, 2048, d_yp), o_copy(3, yp, 2048, 2048, d_ym)]

    def o_fourth_in():
        return [o_copy(2, y2, 0, 2048), o_copy(3, y2, 2048, 2048)]

    @pl.when(mine)
    def _():
        def start(r, _):
            tok_local(r).start()
            return 0
        lax.fori_loop(0, NC, start, 0)
        for n in range(3):
            w_local(n).start()

    def send_inputs(k):
        for step in range(4):
            @pl.when(jnp.logical_and(other, k == 2 * step))
            def _(step=step):
                for r in range(4 * step, 4 * step + 4):
                    tok_remote(r).start()
                if step < 3:
                    w_first(step).start()
        for step in range(3):
            @pl.when(jnp.logical_and(other, k == 2 * step + 3))
            def _(step=step):
                w_first(step).wait_recv()
                for copy in w_second(step):
                    copy.start()

            @pl.when(jnp.logical_and(other, k == 2 * step + 5))
            def _(step=step):
                for copy, forward in zip(w_second_in(step), w_third(step)):
                    copy.wait_recv()
                    forward.start()

        @pl.when(k == 0)
        def _():
            for d in range(4):
                o_first(d).start()

        @pl.when(k == 2)
        def _():
            o_first(0).wait()
            for d in (1, 2, 3):
                o_first(d).wait_recv()

        @pl.when(jnp.logical_and(k >= 2, k < 10))
        def _():
            o_part(0, x, xn, (k - 2) * 128, 128).start()
            o_part(1, x, xc, (k - 2) * 128, 128).start()

        @pl.when(jnp.logical_and(k >= 4, k < 12))
        def _():
            o_part(0, xn, xn, (k - 4) * 128, 128).wait_recv()
            o_part(2, xn, xc, (k - 4) * 128, 128).start()

        def third(x_):
            for copy in o_third(x_):
                copy.start()

        @pl.when(k == 8)
        def _():
            third(x)

        @pl.when(k == 12)
        def _():
            third(xn)
            o_part(1, xc, xn).wait_recv()
            third(xc)

        @pl.when(k == 14)
        def _():
            o_part(2, xd, xn).wait_recv()
            third(xd)

    ALL, XF, ZF, Z1, Z2 = (0, CH), (0, RX), (RX, RZ), (RX, HZ), (RX + HZ, RZ - HZ)

    def gather(r, k, rows, column, device=None):
        part = slot(r, column, *rows)
        return remote(part, part, g_s.at[r], g_r.at[r, k], d_sib if device is None else device)

    def to_sibling(r, piece):
        gather(r, SIB, ALL, cols[piece]).start()

    c_long, c_short = jnp.where(c == 0, c_m, c_p), jnp.where(c == 0, c_p, c_m)
    d_long, d_short = at(y, c, x, jnp.where(c == 0, zp, zm)), at(y, c, x, jnp.where(c == 0, zm, zp))

    def hop0(r):
        tok_wait(r)
        gather(r, 0, XF, c_own, d_xn).start()
        gather(r, 8, ZF, c_own, d_zp).start()
        gather(r, 9, ZF, c_own, d_zm).start()
        gather(r, 1, XF, c_own, d_zp).start()
        gather(r, 2, XF, c_own, d_zm).start()
        gather(r, 7, ZF, c_own, d_xn).start()
        to_sibling(r, 0)

    def hop1(r):
        gather(r, 0, XF, c_x).wait_recv()
        gather(r, 3, XF, c_x, d_zp).start()
        gather(r, 4, XF, c_x, d_zm).start()
        gather(r, 8, ZF, c_m).wait_recv()
        gather(r, 12, ZF, c_m, d_xn).start()
        gather(r, 9, ZF, c_p).wait_recv()
        gather(r, 13, ZF, c_p, d_xn).start()
        gather(r, 10, Z1, c_long, d_long).start()
        gather(r, 11, Z2, c_short, d_short).start()
        gather(r, 1, XF, c_m).wait_recv()
        gather(r, 5, XF, c_m, d_zp).start()
        to_sibling(r, 2)
        gather(r, 2, XF, c_p).wait_recv()
        to_sibling(r, 3)
        gather(r, 7, ZF, c_x).wait_recv()
        to_sibling(r, 1)

    def hop2(r):
        gather(r, 4, XF, c_xp).wait_recv()
        gather(r, 6, XF, c_xp, d_zm).start()
        gather(r, 10, Z1, c_2).wait_recv()
        gather(r, 11, Z2, c_2).wait_recv()
        gather(r, 14, ZF, c_2, d_xn).start()
        gather(r, 3, XF, c_xm).wait_recv()
        gather(r, 12, ZF, c_xm).wait_recv()
        to_sibling(r, 4)
        gather(r, 13, ZF, c_xp).wait_recv()
        to_sibling(r, 5)

    def hop3(r):
        gather(r, 5, XF, c_2).wait_recv()
        to_sibling(r, 6)
        gather(r, 6, XF, c_x2).wait_recv()
        gather(r, 14, ZF, c_x2).wait_recv()
        to_sibling(r, 7)

    def heads(n):
        return slice(n * DH, (n + 1) * DH)

    def state_copy(to):
        to_y, to_half = div(to, 2), rem(to, 2)
        to_x = jnp.where(to_half == half, x, xc)
        return remote(tot, carry.at[shard], t_s.at[to], t_r.at[shard], at(to_y, c, to_x, z))

    def project(r, n):
        qkv[n] = jnp.dot(wide_rows(xg, r), w[n], preferred_element_type=F32).astype(BF)

    def step_key(r):
        for half_block in range(2):
            eight = xg.at[r, pl.ds(0, 4)]
            remote(eight, eight, g_s.at[2 * r], g_r.at[2 * r + half_block, SIB], d_sib).wait_recv()
        project(r, 1)

    def step_value(r):
        project(r, 2)
        for n in range(2):
            total = run[n]
            st[r, n] = total
            run[n] = total + lax.dot_general(
                qkv[1, :, heads(n)], qkv[2, :, heads(n)], (((0,), (0,)), ((), ())), preferred_element_type=F32)

        @pl.when(r == NB - 1)
        def _():
            tot[...] = run[...].astype(BF)

            def send(to, _):
                state_copy(to).start()
                return 0
            lax.fori_loop(shard + 1, 8, send, 0)

    def step_query(r):
        project(r, 0)
        q[r] = qkv[0]

    def step_attend(r):
        causal = (lax.broadcasted_iota(jnp.int32, (BLOCK, BLOCK), 0)
                  >= lax.broadcasted_iota(jnp.int32, (BLOCK, BLOCK), 1))
        for n in range(2):
            scores = lax.dot_general(
                qkv[0, :, heads(n)], qkv[1, :, heads(n)], (((1,), (1,)), ((), ())), preferred_element_type=F32)
            scores = jnp.where(causal, scores, 0.0).astype(BF)
            intra[r, :, heads(n)] = jnp.dot(scores, qkv[2, :, heads(n)], preferred_element_type=F32)

    run[...] = jnp.zeros_like(run)

    send_inputs(0)
    for r in range(AHEAD):
        hop0(r)

    def done(k):
        return jnp.maximum(jnp.minimum(jnp.where(mine, NB, k - LATE + 1), div(k - 3, 2)), 0)

    def round1(k, _):
        block = done(k - 1)
        busy = done(k) > block

        @pl.when(k > 0)
        def _():
            send_inputs(k)

        @pl.when(k < NC - AHEAD)
        def _():
            hop0(k + AHEAD)

        @pl.when(jnp.logical_and(mine, k == 5))
        def _():
            for n in range(3):
                w_local(n).wait()

        @pl.when(jnp.logical_and(other, k == LATE))
        def _():
            for n in range(3):
                for copy in w_third_in(n):
                    copy.wait_recv()

        steps = (step_key, step_value, step_query, step_attend)
        for late, (hop, step) in enumerate(zip((None, hop1, hop2, hop3), steps)):
            if hop is not None:
                @pl.when(jnp.logical_and(k >= late, k < NC + late))
                def _(hop=hop, late=late):
                    hop(k - late)

            @pl.when(busy)
            def _(step=step):
                step(block)
        return 0
    lax.fori_loop(0, NC + 4, round1, 0)

    run[...] = jnp.zeros_like(run)

    def add(k, _):
        remote(tot, carry.at[k], t_s.at[k], t_r.at[k], d_sib).wait_recv()
        run[...] += carry[k].astype(F32)
        return 0
    lax.fori_loop(0, shard, add, 0)

    def lower(r, _):
        low[r] = (st[r] + run[...]).astype(BF)
        return 0
    lax.fori_loop(0, NB, lower, 0)

    for copy, forward in zip(o_third_in(), o_fourth()):
        copy.wait_recv()
        forward.start()

    def attended(r, first):
        rows = pl.ds(pl.multiple_of(first, OC), OC)
        parts = []
        for n in range(2):
            inter = jnp.dot(q[r, rows, heads(n)], low[r, n], preferred_element_type=F32)
            parts.append(((inter + intra[r, rows, heads(n)]) * scale).astype(BF))
        return jnp.concatenate(parts, axis=1)

    def slot3(m, piece):
        return ag.at[m, piece]

    def spread(m, k, column, device=None):
        part = slot3(m, column)
        return remote(part, part, a_s.at[m], a_r.at[m, k], d_sib if device is None else device)

    def spread_sibling(m, piece):
        spread(m, SIB3, cols[piece]).start()

    def hand_over(m):
        return remote(attn.at[m], slot3(m, c_own), a_s.at[m], a_r.at[m, 0], d_xn)

    def turn0(m):
        r, first = 2 * div(m, 2), rem(m, 2) * OC
        slot3(m, c_own)[...] = attended(r + xi, first)
        spread(m, 1, c_own, d_zp).start()
        spread(m, 2, c_own, d_zm).start()
        attn[m] = attended(r + 1 - xi, first)
        hand_over(m).start()
        spread_sibling(m, 0)

    def turn1(m):
        spread(m, 0, c_x).wait_recv()
        spread(m, 3, c_x, d_zp).start()
        spread(m, 4, c_x, d_zm).start()
        spread_sibling(m, 1)
        spread(m, 1, c_m).wait_recv()
        spread(m, 5, c_m, d_zp).start()
        spread_sibling(m, 2)
        spread(m, 2, c_p).wait_recv()
        spread_sibling(m, 3)

    def turn2(m):
        spread(m, 4, c_xp).wait_recv()
        spread(m, 6, c_xp, d_zm).start()
        spread_sibling(m, 5)
        spread(m, 3, c_xm).wait_recv()
        spread_sibling(m, 4)

    def turn3(m):
        spread(m, 5, c_2).wait_recv()
        spread_sibling(m, 6)
        spread(m, 6, c_x2).wait_recv()
        spread_sibling(m, 7)

    def out_rows(m):
        return pl.ds(pl.multiple_of((2 * div(m, 2) + xi) * BLOCK + rem(m, 2) * OC, OC), OC)

    def result(m, n):
        return remote(outb.at[m, n], out.at[out_rows(m)], r_s.at[m, n], r_r.at[0],
                      at(y, half, 2 * c + n, z))

    def result_local(m, n):
        return pltpu.make_async_copy(outb.at[m, n], out.at[out_rows(m)], r_r.at[0])

    def turn4(m):
        eight = ag.at[m, pl.ds(0, 8)]
        remote(eight, eight, a_s.at[m], a_r.at[m, SIB3], d_sib).wait_recv()

        def multiply(n, _):
            outb[m, n] = jnp.dot(wide_rows(ag, m), wog[n], preferred_element_type=F32).astype(BF)
            here = jnp.logical_and(mine, n == xi)

            @pl.when(here)
            def _():
                result_local(m, n).start()

            @pl.when(jnp.logical_not(here))
            def _():
                result(m, n).start()
            return 0
        lax.fori_loop(0, 2, multiply, 0)

    for m in range(AHEAD3):
        turn0(m)

    def round3(k, _):
        @pl.when(k < NO - AHEAD3)
        def _():
            turn0(k + AHEAD3)

        @pl.when(jnp.logical_and(k >= 1, k < NO + 1))
        def _():
            turn1(k - 1)

        @pl.when(jnp.logical_and(k >= 2, k < NO + 2))
        def _():
            turn2(k - 2)

        @pl.when(jnp.logical_and(k >= 3, k < NO + 3))
        def _():
            turn3(k - 3)

        @pl.when(k == 4)
        def _():
            for copy in o_fourth_in():
                copy.wait_recv()

        @pl.when(k >= 4)
        def _():
            turn4(k - 4)
        return 0
    lax.fori_loop(0, NO + 4, round3, 0)

    def sent1(r, _):
        part = xg.at[0, pl.ds(0, 15), pl.ds(0, CH)]
        pltpu.make_async_copy(part, part, g_s.at[r]).wait()
        return 0
    lax.fori_loop(0, NC, sent1, 0)

    def sent3(m, _):
        part = ag.at[m, pl.ds(0, 15)]
        pltpu.make_async_copy(part, part, a_s.at[m]).wait()
        return 0
    lax.fori_loop(0, NO, sent3, 0)

    def sent_result(m, _):
        for n in range(2):
            @pl.when(jnp.logical_not(jnp.logical_and(mine, n == xi)))
            def _(n=n):
                result(m, n).wait_send()
        return 0
    lax.fori_loop(0, NO, sent_result, 0)

    @pl.when(other)
    def _():
        for r in range(NC):
            tok_remote(r).wait_send()
        for n in range(3):
            for copy in [w_first(n)] + w_second(n) + w_third(n):
                copy.wait_send()
    for copy in [o_first(d) for d in (1, 2, 3)] + [o_part(k, x, xn) for k in range(3)] + o_third_out() + o_fourth():
        copy.wait_send()

    def sent_state(to, _):
        state_copy(to).wait_send()
        return 0
    lax.fori_loop(shard + 1, 8, sent_state, 0)

    pltpu.make_async_copy(tok, out, r_r.at[0]).wait()


def local(scale, tokens, w_query, w_key, w_value, w_output):
    rows, feat = tokens.shape
    wide = w_query.shape[0]
    dma, vmem = pltpu.SemaphoreType.DMA, pltpu.VMEM
    return pl.pallas_call(
        lambda *refs: kernel(scale, *refs),
        out_shape=jax.ShapeDtypeStruct((rows, feat), BF),
        in_specs=[pl.BlockSpec(memory_space=pl.ANY)] * 5,
        out_specs=pl.BlockSpec(memory_space=pl.ANY),
        scratch_shapes=[
            vmem((NB, 16, BLOCK, FEAT), BF),
            vmem((3, wide, FEAT), BF),
            vmem((NB, BLOCK, FEAT), BF),
            vmem((3, BLOCK, FEAT), BF),
            vmem((NB, BLOCK, FEAT), F32),
            vmem((NB, 2, DH, DH), F32),
            vmem((2, DH, DH), F32),
            vmem((2, DH, DH), BF),
            vmem((8, 2, DH, DH), BF),
            vmem((NB, 2, DH, DH), BF),
            vmem((NO, OC, FEAT), BF),
            vmem((NO, 16, OC, FEAT), BF),
            vmem((2, wide, FEAT), BF),
            vmem((NO, 2, OC, FEAT), BF),
            dma((NC,)), dma((NC,)),
            dma((3,)),
            dma((3,)), dma((3,)),
            dma((3, 4)), dma((3, 4)),
            dma((4,)), dma((4,)),
            dma((3,)), dma((3, 9)),
            dma((4,)), dma((4,)),
            dma((NC,)), dma((NC, 16)),
            dma((8,)), dma((8,)),
            dma((NO,)), dma((NO, 8)),
            dma((NO, 2)), dma((1,)),
        ],
        name="layer",
        cost_estimate=pl.CostEstimate(flops=18_000_000_000, bytes_accessed=12 << 20, transcendentals=0),
        compiler_params=pltpu.CompilerParams(
            collective_id=0, has_side_effects=True, vmem_limit_bytes=56 << 20),
    )(tokens, w_query, w_key, w_value, w_output)


def solution(mesh):
    scale = 1.0 / math.sqrt(DH * 16384)
    in_specs = (
        P("seq", "tensor"),
        P(None, "tensor"),
        P(None, "tensor"),
        P(None, "tensor"),
        P("tensor", None),
    )
    return jax.shard_map(
        lambda *args: local(scale, *args),
        mesh=mesh, in_specs=in_specs, out_specs=P("seq", "tensor"), check_vma=False)
```

time: 161 us -> 144 us (0.89)
  Pallas kernels: 159 us -> 141 us
    pallas_call x1, Pallas kernels: 159 us -> 141 us  [local(): pl.pallas_call(lambda *refs: kernel(scale, *refs), out_shape=jax.ShapeDty...]
where the time goes in v2:
time: 144 us; the launch traced here: 143 us
  Pallas kernels  141 us (98%)
  local copies, waits for them, and re-layouts  2.26 us (2%)
    pallas_call x1, Pallas kernels, local(): pl.pallas_call(lambda *refs: kernel(scale, *refs), out_shape=jax.ShapeDty...  141 us

profile of v2, /device:TPU:17, one launch (start us, length us, event | category | flops | bytes accessed | tf_op | source)
XLA Modules:
  0.0 143.3 jit_solution(11748729802453001513)
XLA Ops:
  0.0 141.0 %layer.1 = bf16[2048,256]{1,0:T(8,128)(2,1)} custom-call(bf16[2048,256]{1,0:T(8,128)(2,1)} %refs_0_.1, bf16[4096,256]{1,0:T(8,128)(2,1)} %refs_1_.1, bf16[4096,256]{1,0:T(8,128)(2,1)} %refs_2_.1, bf16[4096,256]{1,0:T(8,128)(2,1)} %refs_3_.1, bf16[256,4096]{1,0:T(8,128)(2,1)} %refs_4_.1), custom_call_target="tpu_custom_call" | custom-call | flops 17999998976 | bytes 12582912 | tf_op jit(solution)/shard_map/layer/pallas_call | solution.py:555
  141.1 2.3 %copy.7 = bf16[2048,256]{1,0:T(8,128)(2,1)} copy(bf16[2048,256]{1,0:T(8,128)(2,1)} %layer.1) | data formatting | bytes 2097152

commit v3 on v2

--- a/solution.py
+++ b/solution.py
@@ -23,6 +23,10 @@
 SIB = 15
 SIB3 = 7
 AHEAD = 1
+WP = 128
+FULL = 6
+OP = 64
+THIRD = 12
 LATE = 12
 AHEAD3 = 1
 
@@ -40,7 +44,7 @@
 
 def kernel(scale, tok, wq, wk, wv, wo, out,
            xg, w, q, qkv, intra, st, run, tot, carry, low, attn, ag, wog, outb,
-           pre_s, pre_r, w_l, w1_s, w1_r, w2_s, w2_r, o1_s, o1_r, o2_s, o2_r, o3_s, o3_r,
+           pre_s, pre_r, w_l, w1_s, w1_r, w2_s, w2_r, w3_s, w3_r, o1_s, o1_r, o2_s, o2_r, o3_s, o3_r,
            g_s, g_r, t_s, t_r, a_s, a_r, r_s, r_r):
     div, rem = lax.div, lax.rem
     seq, ten = lax.axis_index("seq"), lax.axis_index("tensor")
@@ -97,27 +101,27 @@
     def w_local(n):
         return pltpu.make_async_copy(w_hbm[n], w.at[n], w_l.at[n])
 
-    def w_first(n):
-        return remote(w_hbm[n].at[quarter], w.at[n, quarter], w1_s.at[n], w1_r.at[n], d_part)
+    def w_rows(y_, i, first=0, count=WP):
+        return pl.ds(pl.multiple_of(y_ * 1024 + i * WP + first, 16), count)
+
+    def w_first(n, i):
+        rows = w_rows(y, i)
+        return remote(w_hbm[n].at[rows], w.at[n, rows], w1_s.at[0], w1_r.at[i], at(y, c, xc, z))
 
     yp, ym, y2 = rem(y + 1, 4), rem(y + 3, 4), rem(y + 2, 4)
     d_yp, d_ym = at(yp, c, x, z), at(ym, c, x, z)
 
-    def w_copy(n, k, y_, first, count, device=None):
-        rows = pl.ds(pl.multiple_of(y_ * 1024 + first, 16), count)
-        return remote(w.at[n, rows], w.at[n, rows], w2_s.at[n, k], w2_r.at[n, k], d_yp if device is None else device)
-
-    def w_second(n):
-        return [w_copy(n, 0, y, 0, 1024, d_yp), w_copy(n, 1, y, 0, 1024, d_ym)]
-
-    def w_second_in(n):
-        return [w_copy(n, 0, ym, 0, 1024), w_copy(n, 1, yp, 0, 1024)]
-
-    def w_third(n):
-        return [w_copy(n, 2, ym, 0, 512, d_yp), w_copy(n, 3, yp, 512, 512, d_ym)]
-
-    def w_third_in(n):
-        return [w_copy(n, 2, y2, 0, 512), w_copy(n, 3, y2, 512, 512)]
+    def w_second(n, i):
+        part = w.at[n, w_rows(y, i)]
+        return [remote(part, part, w2_s.at[k], w2_r.at[k, i], to) for k, to in enumerate((d_yp, d_ym))]
+
+    def w_third(n, i):
+        parts = w.at[n, w_rows(ym, i, 0, WP // 2)], w.at[n, w_rows(yp, i, WP // 2, WP // 2)]
+        return [remote(part, part, w3_s.at[k], w3_r.at[k], to) for k, (part, to) in enumerate(zip(parts, (d_yp, d_ym)))]
+
+    def w_wait(rows, semaphore):
+        part = w.at[:, pl.ds(0, rows)]
+        pltpu.make_async_copy(part, part, semaphore).wait()
 
     o_cols = pl.ds(pl.multiple_of(rem(y, 2) * DH, DH), DH)
     o_blk = div(y, 2)
@@ -133,19 +137,19 @@
         to = rem(z + d, 4)
         return remote(o_source(to), o_mine, o1_s.at[d], o1_r.at[d], at(y, c, x, to))
 
-    def o_part(k, x_, to, first=0, count=1024):
-        rows = pl.ds(pl.multiple_of(x_ * 1024 + first, 16), count)
+    def o_part(k, x_, to, i, count=OP):
+        rows = pl.ds(pl.multiple_of(x_ * 1024 + i * OP, OP), count)
         part = wog.at[o_blk, rows, o_cols]
-        place = div(first, 128) if k == 0 and count < 1024 else 8
-        return remote(part, part, o2_s.at[k], o2_r.at[k, place], at(y, c, to, z))
+        return remote(part, part, o2_s.at[k], o2_r.at[k, i], at(y, c, to, z))
 
     def o_copy(k, y_, first, count, device=None):
         rows, columns = pl.ds(pl.multiple_of(first, 16), count), pl.ds(pl.multiple_of(rem(y_, 2) * DH, DH), DH)
         part = wog.at[div(y_, 2), rows, columns]
         return remote(part, part, o3_s.at[k], o3_r.at[k], d_yp if device is None else device)
 
-    def o_third(x_):
-        return [o_copy(0, y, x_ * 1024, 1024, d_yp), o_copy(1, y, x_ * 1024, 1024, d_ym)]
+    def o_third(x_, i):
+        first = x_ * 1024 + i * WP
+        return [o_copy(0, y, first, WP, d_yp), o_copy(1, y, first, WP, d_ym)]
 
     def o_third_out():
         return [o_copy(0, y, 0, 4096, d_yp), o_copy(1, y, 0, 4096, d_ym)]
@@ -153,8 +157,11 @@
     def o_third_in():
         return [o_copy(0, ym, 0, 4096), o_copy(1, yp, 0, 4096)]
 
-    def o_fourth():
-        return [o_copy(2, ym, 0, 2048, d_yp), o_copy(3, yp, 2048, 2048, d_ym)]
+    def o_fourth(i):
+        return [o_copy(2, ym, i * WP, WP, d_yp), o_copy(3, yp, 2048 + i * WP, WP, d_ym)]
+
+    def o_fourth_out():
+        return [o_copy(2, ym, 0, 2048), o_copy(3, yp, 2048, 2048)]
 
     def o_fourth_in():
         return [o_copy(2, y2, 0, 2048), o_copy(3, y2, 2048, 2048)]
@@ -165,7 +172,7 @@
             tok_local(r).start()
             return 0
         lax.fori_loop(0, NC, start, 0)
-        for n in range(3):
+        for n in (1, 2, 0):
             w_local(n).start()
 
     def send_inputs(k):
@@ -174,20 +181,25 @@
             def _(step=step):
                 for r in range(4 * step, 4 * step + 4):
                     tok_remote(r).start()
-                if step < 3:
-                    w_first(step).start()
-        for step in range(3):
-            @pl.when(jnp.logical_and(other, k == 2 * step + 3))
-            def _(step=step):
-                w_first(step).wait_recv()
-                for copy in w_second(step):
+        @pl.when(jnp.logical_and(mine, k < 8))
+        def _():
+            for n in (1, 2, 0):
+                w_first(n, k).start()
+
+        @pl.when(jnp.logical_and(other, jnp.logical_and(k >= 2, k < 10)))
+        def _():
+            w_wait(WP, w1_r.at[k - 2])
+            for n in (1, 2, 0):
+                for copy in w_second(n, k - 2):
                     copy.start()
 
-            @pl.when(jnp.logical_and(other, k == 2 * step + 5))
-            def _(step=step):
-                for copy, forward in zip(w_second_in(step), w_third(step)):
-                    copy.wait_recv()
-                    forward.start()
+        @pl.when(jnp.logical_and(other, jnp.logical_and(k >= 4, k < 12)))
+        def _():
+            for d in range(2):
+                w_wait(WP, w2_r.at[d, k - 4])
+            for n in (1, 2, 0):
+                for copy in w_third(n, k - 4):
+                    copy.start()
 
         @pl.when(k == 0)
         def _():
@@ -200,34 +212,41 @@
             for d in (1, 2, 3):
                 o_first(d).wait_recv()
 
-        @pl.when(jnp.logical_and(k >= 2, k < 10))
-        def _():
-            o_part(0, x, xn, (k - 2) * 128, 128).start()
-            o_part(1, x, xc, (k - 2) * 128, 128).start()
-
-        @pl.when(jnp.logical_and(k >= 4, k < 12))
-        def _():
-            o_part(0, xn, xn, (k - 4) * 128, 128).wait_recv()
-            o_part(2, xn, xc, (k - 4) * 128, 128).start()
-
-        def third(x_):
-            for copy in o_third(x_):
+        def third(x_, i):
+            for copy in o_third(x_, i):
                 copy.start()
 
-        @pl.when(k == 8)
-        def _():
-            third(x)
-
-        @pl.when(k == 12)
-        def _():
-            third(xn)
-            o_part(1, xc, xn).wait_recv()
-            third(xc)
-
-        @pl.when(k == 14)
-        def _():
-            o_part(2, xd, xn).wait_recv()
-            third(xd)
+        @pl.when(jnp.logical_and(k >= 2, k < 18))
+        def _():
+            o_part(0, x, xn, k - 2).start()
+            o_part(1, x, xc, k - 2).start()
+
+        @pl.when(jnp.logical_and(k >= 4, k < 20))
+        def _():
+            o_part(0, xn, xn, k - 4).wait_recv()
+            o_part(2, xn, xc, k - 4).start()
+
+        @pl.when(k >= THIRD)
+        def _():
+            i = k - THIRD
+            third(x, i)
+            third(xn, i)
+            for half_piece in range(2):
+                o_part(1, xc, xn, 2 * i + half_piece).wait_recv()
+            third(xc, i)
+
+        @pl.when(k >= THIRD + 1)
+        def _():
+            third_last(k - THIRD - 1)
+
+    def third(x_, i):
+        for copy in o_third(x_, i):
+            copy.start()
+
+    def third_last(i):
+        for half_piece in range(2):
+            o_part(2, xd, xn, 2 * i + half_piece).wait_recv()
+        third(xd, i)
 
     ALL, XF, ZF, Z1, Z2 = (0, CH), (0, RX), (RX, RZ), (RX, HZ), (RX + HZ, RZ - HZ)
 
@@ -363,9 +382,8 @@
 
         @pl.when(jnp.logical_and(other, k == LATE))
         def _():
-            for n in range(3):
-                for copy in w_third_in(n):
-                    copy.wait_recv()
+            for d in range(2):
+                w_wait(512, w3_r.at[d])
 
         steps = (step_key, step_value, step_query, step_attend)
         for late, (hop, step) in enumerate(zip((None, hop1, hop2, hop3), steps)):
@@ -380,6 +398,8 @@
         return 0
     lax.fori_loop(0, NC + 4, round1, 0)
 
+    third_last(7)
+
     run[...] = jnp.zeros_like(run)
 
     def add(k, _):
@@ -392,10 +412,6 @@
         low[r] = (st[r] + run[...]).astype(BF)
         return 0
     lax.fori_loop(0, NB, lower, 0)
-
-    for copy, forward in zip(o_third_in(), o_fourth()):
-        copy.wait_recv()
-        forward.start()
 
     def attended(r, first):
         rows = pl.ds(pl.multiple_of(first, OC), OC)
@@ -499,14 +515,29 @@
         def _():
             turn3(k - 3)
 
-        @pl.when(k == 4)
+        @pl.when(k == 1)
+        def _():
+            for copy in o_third_in():
+                copy.wait_recv()
+
+        @pl.when(jnp.logical_and(k >= 1, k < 5))
+        def _():
+            for i in range(4):
+                for copy in o_fourth(4 * k - 4 + i):
+                    copy.start()
+
+        @pl.when(k == FULL)
         def _():
             for copy in o_fourth_in():
                 copy.wait_recv()
 
-        @pl.when(k >= 4)
-        def _():
-            turn4(k - 4)
+        def done3(k_):
+            return jnp.maximum(jnp.minimum(k_ - 3, 2 * (k_ - FULL + 1)), 0)
+
+        def multiply(m, _):
+            turn4(m)
+            return 0
+        lax.fori_loop(done3(k - 1), done3(k), multiply, 0)
         return 0
     lax.fori_loop(0, NO + 4, round3, 0)
 
@@ -534,10 +565,14 @@
     def _():
         for r in range(NC):
             tok_remote(r).wait_send()
-        for n in range(3):
-            for copy in [w_first(n)] + w_second(n) + w_third(n):
-                copy.wait_send()
-    for copy in [o_first(d) for d in (1, 2, 3)] + [o_part(k, x, xn) for k in range(3)] + o_third_out() + o_fourth():
+        for d in range(2):
+            w_wait(1024, w2_s.at[d])
+            w_wait(512, w3_s.at[d])
+
+    @pl.when(mine)
+    def _():
+        w_wait(1024, w1_s.at[0])
+    for copy in [o_first(d) for d in (1, 2, 3)] + [o_part(k, x, xn, 0, 1024) for k in range(3)] + o_third_out() + o_fourth_out():
         copy.wait_send()
 
     def sent_state(to, _):
@@ -574,10 +609,11 @@
             vmem((NO, 2, OC, FEAT), BF),
             dma((NC,)), dma((NC,)),
             dma((3,)),
-            dma((3,)), dma((3,)),
-            dma((3, 4)), dma((3, 4)),
+            dma((1,)), dma((8,)),
+            dma((2,)), dma((2, 8)),
+            dma((2,)), dma((2,)),
             dma((4,)), dma((4,)),
-            dma((3,)), dma((3, 9)),
+            dma((3,)), dma((3, 16)),
             dma((4,)), dma((4,)),
             dma((NC,)), dma((NC, 16)),
             dma((8,)), dma((8,)),

time: 144 us -> 138 us (0.958)
  Pallas kernels: 141 us -> 135 us
    pallas_call x1, Pallas kernels: 141 us -> 135 us  [local(): pl.pallas_call(lambda *refs: kernel(scale, *refs), out_shape=jax.ShapeDty...]
where the time goes in v3:
time: 138 us
  Pallas kernels  135 us (98%)
  local copies, waits for them, and re-layouts  2.26 us (2%)
    pallas_call x1, Pallas kernels, local(): pl.pallas_call(lambda *refs: kernel(scale, *refs), out_shape=jax.ShapeDty...  135 us

profile of v3, /device:TPU:17, one launch (start us, length us, event | category | flops | bytes accessed | tf_op | source)
XLA Modules:
  0.0 137.6 jit_solution(13823226467302219942)
XLA Ops:
  0.0 135.4 %layer.1 = bf16[2048,256]{1,0:T(8,128)(2,1)} custom-call(bf16[2048,256]{1,0:T(8,128)(2,1)} %refs_0_.1, bf16[4096,256]{1,0:T(8,128)(2,1)} %refs_1_.1, bf16[4096,256]{1,0:T(8,128)(2,1)} %refs_2_.1, bf16[4096,256]{1,0:T(8,128)(2,1)} %refs_3_.1, bf16[256,4096]{1,0:T(8,128)(2,1)} %refs_4_.1), custom_call_target="tpu_custom_call" | custom-call | flops 17999998976 | bytes 12582912 | tf_op jit(solution)/shard_map/layer/pallas_call | solution.py:590
  135.4 2.3 %copy.7 = bf16[2048,256]{1,0:T(8,128)(2,1)} copy(bf16[2048,256]{1,0:T(8,128)(2,1)} %layer.1) | data formatting | bytes 2097152

commit v4 on v3

--- a/solution.py
+++ b/solution.py
@@ -22,7 +22,7 @@
 FEAT = 256
 SIB = 15
 SIB3 = 7
-AHEAD = 1
+AHEAD = 0
 WP = 128
 FULL = 6
 OP = 64
@@ -77,7 +77,6 @@
                   at(rem(y + d, 4), c, x, z), at(rem(y + d, 4), c, xc, z)]
     for peer in peers:
         pl.semaphore_signal(barrier, inc=1, device_id=peer, device_id_type=pl.DeviceIdType.MESH)
-    pl.semaphore_wait(barrier, len(peers))
 
     w_hbm = (wq, wk, wv)
     quarter = pl.ds(pl.multiple_of(y * 1024, 1024), 1024)
@@ -175,12 +174,18 @@
         for n in (1, 2, 0):
             w_local(n).start()
 
+    pl.semaphore_wait(barrier, len(peers))
+
     def send_inputs(k):
-        for step in range(4):
-            @pl.when(jnp.logical_and(other, k == 2 * step))
-            def _(step=step):
-                for r in range(4 * step, 4 * step + 4):
-                    tok_remote(r).start()
+        @pl.when(jnp.logical_and(other, k == 0))
+        def _():
+            for r in range(4):
+                tok_remote(r).start()
+
+        @pl.when(jnp.logical_and(other, jnp.logical_and(k >= 1, k < NC - 3)))
+        def _():
+            tok_remote(k + 3).start()
+
         @pl.when(jnp.logical_and(mine, k < 8))
         def _():
             for n in (1, 2, 0):

time: 138 us -> 136 us (0.986)
  Pallas kernels: 135 us -> 133 us
    pallas_call x1, Pallas kernels: 135 us -> 133 us  [local(): pl.pallas_call(lambda *refs: kernel(scale, *refs), out_shape=jax.ShapeDty...]
where the time goes in v4:
time: 136 us; the launch traced here: 135 us
  Pallas kernels  133 us (98%)
  local copies, waits for them, and re-layouts  2.26 us (2%)
    pallas_call x1, Pallas kernels, local(): pl.pallas_call(lambda *refs: kernel(scale, *refs), out_shape=jax.ShapeDty...  133 us

profile of v4, /device:TPU:17, one launch (start us, length us, event | category | flops | bytes accessed | tf_op | source)
XLA Modules:
  0.0 135.4 jit_solution(10414473211153639206)
XLA Ops:
  0.0 133.1 %layer.1 = bf16[2048,256]{1,0:T(8,128)(2,1)} custom-call(bf16[2048,256]{1,0:T(8,128)(2,1)} %refs_0_.1, bf16[4096,256]{1,0:T(8,128)(2,1)} %refs_1_.1, bf16[4096,256]{1,0:T(8,128)(2,1)} %refs_2_.1, bf16[4096,256]{1,0:T(8,128)(2,1)} %refs_3_.1, bf16[256,4096]{1,0:T(8,128)(2,1)} %refs_4_.1), custom_call_target="tpu_custom_call" | custom-call | flops 17999998976 | bytes 12582912 | tf_op jit(solution)/shard_map/layer/pallas_call | solution.py:595
  133.1 2.3 %copy.7 = bf16[2048,256]{1,0:T(8,128)(2,1)} copy(bf16[2048,256]{1,0:T(8,128)(2,1)} %layer.1) | data formatting | bytes 2097152

commit v5 on v4

--- a/solution.py
+++ b/solution.py
@@ -24,7 +24,7 @@
 SIB3 = 7
 AHEAD = 0
 WP = 128
-FULL = 6
+FULL = 7
 OP = 64
 THIRD = 12
 LATE = 12
@@ -441,11 +441,11 @@
 
     def turn0(m):
         r, first = 2 * div(m, 2), rem(m, 2) * OC
+        attn[m] = attended(r + 1 - xi, first)
+        hand_over(m).start()
         slot3(m, c_own)[...] = attended(r + xi, first)
         spread(m, 1, c_own, d_zp).start()
         spread(m, 2, c_own, d_zm).start()
-        attn[m] = attended(r + 1 - xi, first)
-        hand_over(m).start()
         spread_sibling(m, 0)
 
     def turn1(m):

time: 136 us -> 136 us (level)
  no operation moved by 1% of the time
where the time goes in v5:
time: 136 us
  Pallas kernels  134 us (99%)
  local copies, waits for them, and re-layouts  2.26 us (2%)
    pallas_call x1, Pallas kernels, local(): pl.pallas_call(lambda *refs: kernel(scale, *refs), out_shape=jax.ShapeDty...  134 us

profile of v5, /device:TPU:17, one launch (start us, length us, event | category | flops | bytes accessed | tf_op | source)
XLA Modules:
  0.0 136.3 jit_solution(8698006704463832028)
XLA Ops:
  0.0 134.0 %layer.1 = bf16[2048,256]{1,0:T(8,128)(2,1)} custom-call(bf16[2048,256]{1,0:T(8,128)(2,1)} %refs_0_.1, bf16[4096,256]{1,0:T(8,128)(2,1)} %refs_1_.1, bf16[4096,256]{1,0:T(8,128)(2,1)} %refs_2_.1, bf16[4096,256]{1,0:T(8,128)(2,1)} %refs_3_.1, bf16[256,4096]{1,0:T(8,128)(2,1)} %refs_4_.1), custom_call_target="tpu_custom_call" | custom-call | flops 17999998976 | bytes 12582912 | tf_op jit(solution)/shard_map/layer/pallas_call | solution.py:595
  134.0 2.3 %copy.7 = bf16[2048,256]{1,0:T(8,128)(2,1)} copy(bf16[2048,256]{1,0:T(8,128)(2,1)} %layer.1) | data formatting | bytes 2097152
